TPU v7x, 128 devices: a whole 4x4x4 slice. The times are simulated.
128 devices in a mesh: seq: 32 (over y, x, core), head: 4 (over z).
Axes of the slice: x: 4, y: 4, z: 4, core: 2. Of those that a mesh axis runs over, the one named last changes fastest.
Arguments:
- queries: bfloat16 [16384, 8192], P('seq', 'head'), may hold values from -120 to 120
- keys_values: bfloat16 [16384, 2, 1024], P('seq', None, 'head'), may hold values from -6 to 6
- image_kv: bfloat16 [8192, 2, 1024], P('seq', None, 'head'), may hold values from -6 to 6
- image_of: int32 [128], P('seq'), may hold values from 0 to 7
- ancestors: int32 [128, 8], P('seq'), may hold values from 0 to 127, as said below
- counts: int32 [128], P('seq'), may hold values from 0 to 8, as said below
- out_weight: bfloat16 [8192, 4096], P('head'), may hold values from -1.796875 to 1.796875
Outputs:
- projected: bfloat16 [16384, 4096], P('seq', 'head')
Inputs may be any that keep to these rules, and one draw needn't show every extreme that they name: `ancestors`: entries at slots a >= counts[b] are 0. A listed entry is a block id; block id g belongs to the aligned group g // 4 of 4 blocks. The blocks listed for the blocks of one aligned group never belong to that group, and no two of them belong to the same group. `counts`: in every draw some block lists the full 8 ancestors.
All inputs are finite; a program needn't handle non-finite values.
Results may differ from a plain program's by a relative error of at most 0.015.
Values may be sent and summed in bfloat16 or wider, within the bound.
A program may use at most 192 MiB of HBM per device.

v0:
```python
import jax
import jax.numpy as jnp
from jax import lax
from jax.sharding import PartitionSpec as P

HEAD_DIM = 128
BS = 128
IMG_TOK = 1024


def attend(query_block, key_rows, value_rows, allowed):
    block_rows = query_block.shape[0]
    kv_heads = key_rows.shape[1] // HEAD_DIM
    grouping = query_block.shape[1] // (kv_heads * HEAD_DIM)
    query_heads = query_block.reshape(block_rows, kv_heads, grouping, HEAD_DIM)
    key_heads = key_rows.reshape(-1, kv_heads, HEAD_DIM)
    value_heads = value_rows.reshape(-1, kv_heads, HEAD_DIM)
    scores = jnp.einsum(
        "rkgd,lkd->kgrl", query_heads, key_heads, preferred_element_type=jnp.float32
    ) * HEAD_DIM ** (-0.5)
    scores = jnp.where(allowed[None, None], scores, -jnp.inf)
    largest = jnp.max(scores, axis=-1, keepdims=True)
    exponent = jnp.exp(scores - largest)
    weights = (exponent / jnp.sum(exponent, axis=-1, keepdims=True)).astype(jnp.bfloat16)
    combined = jnp.einsum(
        "kgrl,lkd->rkgd", weights, value_heads, preferred_element_type=jnp.float32
    )
    return combined.astype(jnp.bfloat16).reshape(block_rows, -1)


def allowed_mask(count, slot_count):
    image_part = jnp.ones((BS, IMG_TOK), dtype=bool)
    slot_live = jnp.arange(slot_count, dtype=jnp.int32) < count
    ancestor_part = jnp.broadcast_to(jnp.repeat(slot_live, BS)[None, :], (BS, slot_count * BS))
    positions = jnp.arange(BS, dtype=jnp.int32)
    own_part = positions[None, :] <= positions[:, None]
    return jnp.concatenate([image_part, ancestor_part, own_part], axis=1)


def body(queries, keys_values, image_kv, image_of, ancestors, counts, out_weight):
    block_count = ancestors.shape[0]
    slot_count = ancestors.shape[1]
    width_kv = keys_values.shape[2]
    images_all = lax.all_gather(image_kv, "seq", axis=0, tiled=True)
    own_blocks = keys_values.reshape(block_count, BS, 2, width_kv)
    everything = lax.all_gather(keys_values, "seq", axis=0, tiled=True)
    ancestor_kv = everything.reshape(-1, BS, 2, width_kv)[ancestors]
    query_blocks = queries.reshape(block_count, BS, -1)

    def one_block(block_items):
        query_block, ancestor_rows, own_rows, image_index, count = block_items
        image_start = image_index * IMG_TOK
        image_rows = lax.dynamic_slice_in_dim(images_all, image_start, IMG_TOK, 0)
        gathered = jnp.concatenate(
            [image_rows, ancestor_rows.reshape(slot_count * BS, 2, width_kv), own_rows], axis=0
        )
        return attend(query_block, gathered[:, 0], gathered[:, 1], allowed_mask(count, slot_count))

    attended = lax.map(one_block, (query_blocks, ancestor_kv, own_blocks, image_of, counts))
    attended = attended.reshape(-1, queries.shape[1])
    partial_value = jnp.dot(attended, out_weight, preferred_element_type=jnp.float32)
    summed = lax.psum(partial_value, "head")
    own_width = partial_value.shape[1] // lax.axis_size("head")
    own_share = lax.dynamic_slice_in_dim(summed, lax.axis_index("head") * own_width, own_width, 1)
    return own_share.astype(jnp.bfloat16)


def solution(mesh):
    in_specs = (
        P("seq", "head"),
        P("seq", None, "head"),
        P("seq", None, "head"),
        P("seq"),
        P("seq", None),
        P("seq"),
        P("head", None),
    )
    out_specs = P("seq", "head")
    return jax.shard_map(body, mesh=mesh, in_specs=in_specs, out_specs=out_specs, check_vma=False)
```

profile of v0, /device:TPU:0, one launch (start us, length us, event | category | flops | bytes accessed | tf_op | source)
XLA Modules:
  0.0 437.1 jit_solution(16189766607916421605)
XLA Ops:
  6.5 1.9 copy.31
  8.5 1.8 copy.30
  10.4 0.7 compare_select_fusion
  11.1 73.4 %all-gather.5.cloned.1.call-done = bf16[16384,2,256]{2,0,1:T(8,128)(2,1)} async-done(((bf16[512,2,256]{2,0,1:T(8,128)(2,1)}), bf16[16384,2,256]{2,0,1:T(8,128)(2,1)}) %all-gather.5.cloned.1.call-update) | async-done | bytes 16777232 | tf_op jit(solution)/shard_map/all_gather | solution.py:46
  84.5 14.0 %copy.32 = bf16[128,128,2,256]{3,1,2,0:T(8,128)(2,1)} copy(bf16[128,128,2,256]{3,1,0,2:T(8,128)(2,1)} %bitcast.73) | data formatting | bytes 33554432 | tf_op jit(solution)/shard_map/reshape | solution.py:47
  98.5 8.6 %gather_fusion = bf16[32,128,2,256]{3,1,2,0:T(8,128)(2,1)} fusion(bf16[128,128,2,256]{3,1,2,0:T(8,128)(2,1)} %copy.32, s32[1024]{0:T(1024)S(1)} %pad_clamp_fusion), kind=kCustom, calls=%fused_computation | custom fusion | bytes 8388736 | tf_op jit(solution)/shard_map/gather | solution.py:47
  107.1 38.5 %all-gather.3.cloned.1.call-done = bf16[8192,2,256]{0,2,1:T(8,128)(2,1)} async-done(((bf16[256,2,256]{0,2,1:T(8,128)(2,1)}), bf16[8192,2,256]{0,2,1:T(8,128)(2,1)}) %all-gather.3.cloned.1.call-update) | async-done | bytes 8388624 | tf_op jit(solution)/shard_map/all_gather | solution.py:44
  145.6 117.3 %while.10 = (s32[]{:T(128)}, bf16[4,128,2048]{2,1,0:T(8,128)(2,1)}, s32[4]{0:T(128)S(1)}, bf16[8192,2,256]{0,2,1:T(8,128)(2,1)}, bf16[4,8,128,2,256]{4,2,3,1,0:T...) while((s32[]{:T(128)}, bf16[4,128,2048]{2,1,0:T(8,128)(2,1)}, ...), condition=%wide.region_3.4_spmd, body=%wide.region_0.3_spmd.sunk | while | flops 2315686144 | bytes 61563880 | solution.py:59
  146.9 1.3 constant_dynamic-slice_fusion.10
  148.2 1.3 constant_dynamic-slice_fusion.9
  149.5 0.8 copy.56
  150.8 1.0 constant_dynamic-slice_fusion.8
  152.2 1.1 constant_dynamic-slice_fusion.11
  154.2 0.6 iota_compare_fusion.5
  155.0 2.1 pad_add_fusion.5
  157.0 9.4 %fusion.31 = (f32[2,8,128]{2,1,0:T(8,128)S(1)}, f32[2,8,128,2176]{2,3,1,0:T(8,128)}) fusion(pred[128,2176]{0,1:T(8,128)(4,1)S(1)} %pad_add_fusion.5, bf16[2176,2,128,1]{0,2,3,1:T(8,128)(2,1)S(1)} %bitcast.71, bf16[128,2,8,128]{0,3,2,1:T(8,128)(2,1)S(1)} %bitcast.75), kind=kOutput, calls=%fused_computation.29.clone.1 | convolution fusion | flops 1158678656 | bytes 19750912 | tf_op jit(solution)/shard_map/while/body/eval_jaxpr/sub | solution.py:23
  166.4 7.5 %fusion.32 = bf16[2,128,8,128]{3,1,2,0:T(8,128)(2,1)S(1)} fusion(bf16[2176,2,128,1]{0,2,3,1:T(8,128)(2,1)S(1)} %bitcast.70, f32[2,8,128,2176]{2,3,1,0:T(8,128)} %get-tuple-element.147, f32[2,8,128]{2,1,0:T(8,128)S(1)} %get-tuple-element.148), kind=kOutput, calls=%fused_computation.12.clone.1 | convolution fusion | flops 1150025728 | bytes 19472384 | tf_op jit(solution)/shard_map/while/body/eval_jaxpr/kgrl,lkd->rkgd/dot_general | solution.py:25
  174.1 0.8 constant_dynamic-update-slice_fusion.2
  176.2 1.3 constant_dynamic-slice_fusion.10
  177.5 1.3 constant_dynamic-slice_fusion.9
  178.8 0.8 copy.56
  180.1 1.0 constant_dynamic-slice_fusion.8
  181.6 1.1 constant_dynamic-slice_fusion.11
  184.3 2.1 pad_add_fusion.5
  186.4 9.4 %fusion.31 = (f32[2,8,128]{2,1,0:T(8,128)S(1)}, f32[2,8,128,2176]{2,3,1,0:T(8,128)}) fusion(pred[128,2176]{0,1:T(8,128)(4,1)S(1)} %pad_add_fusion.5, bf16[2176,2,128,1]{0,2,3,1:T(8,128)(2,1)S(1)} %bitcast.71, bf16[128,2,8,128]{0,3,2,1:T(8,128)(2,1)S(1)} %bitcast.75), kind=kOutput, calls=%fused_computation.29.clone.1 | convolution fusion | flops 1158678656 | bytes 19750912 | tf_op jit(solution)/shard_map/while/body/eval_jaxpr/sub | solution.py:23
  195.8 7.5 %fusion.32 = bf16[2,128,8,128]{3,1,2,0:T(8,128)(2,1)S(1)} fusion(bf16[2176,2,128,1]{0,2,3,1:T(8,128)(2,1)S(1)} %bitcast.70, f32[2,8,128,2176]{2,3,1,0:T(8,128)} %get-tuple-element.147, f32[2,8,128]{2,1,0:T(8,128)S(1)} %get-tuple-element.148), kind=kOutput, calls=%fused_computation.12.clone.1 | convolution fusion | flops 1150025728 | bytes 19472384 | tf_op jit(solution)/shard_map/while/body/eval_jaxpr/kgrl,lkd->rkgd/dot_general | solution.py:25
  203.5 0.8 constant_dynamic-update-slice_fusion.2
  205.5 1.3 constant_dynamic-slice_fusion.10
  206.9 1.3 constant_dynamic-slice_fusion.9
  208.2 0.8 copy.56
  209.4 1.0 constant_dynamic-slice_fusion.8
  210.9 1.1 constant_dynamic-slice_fusion.11
  213.6 2.1 pad_add_fusion.5
  215.7 9.4 %fusion.31 = (f32[2,8,128]{2,1,0:T(8,128)S(1)}, f32[2,8,128,2176]{2,3,1,0:T(8,128)}) fusion(pred[128,2176]{0,1:T(8,128)(4,1)S(1)} %pad_add_fusion.5, bf16[2176,2,128,1]{0,2,3,1:T(8,128)(2,1)S(1)} %bitcast.71, bf16[128,2,8,128]{0,3,2,1:T(8,128)(2,1)S(1)} %bitcast.75), kind=kOutput, calls=%fused_computation.29.clone.1 | convolution fusion | flops 1158678656 | bytes 19750912 | tf_op jit(solution)/shard_map/while/body/eval_jaxpr/sub | solution.py:23
  225.1 7.5 %fusion.32 = bf16[2,128,8,128]{3,1,2,0:T(8,128)(2,1)S(1)} fusion(bf16[2176,2,128,1]{0,2,3,1:T(8,128)(2,1)S(1)} %bitcast.70, f32[2,8,128,2176]{2,3,1,0:T(8,128)} %get-tuple-element.147, f32[2,8,128]{2,1,0:T(8,128)S(1)} %get-tuple-element.148), kind=kOutput, calls=%fused_computation.12.clone.1 | convolution fusion | flops 1150025728 | bytes 19472384 | tf_op jit(solution)/shard_map/while/body/eval_jaxpr/kgrl,lkd->rkgd/dot_general | solution.py:25
  232.8 0.8 constant_dynamic-update-slice_fusion.2
  234.9 1.3 constant_dynamic-slice_fusion.10
  236.2 1.3 constant_dynamic-slice_fusion.9
  237.5 0.8 copy.56
  238.8 1.0 constant_dynamic-slice_fusion.8
  240.2 1.1 constant_dynamic-slice_fusion.11
  243.0 2.1 pad_add_fusion.5
  245.0 9.4 %fusion.31 = (f32[2,8,128]{2,1,0:T(8,128)S(1)}, f32[2,8,128,2176]{2,3,1,0:T(8,128)}) fusion(pred[128,2176]{0,1:T(8,128)(4,1)S(1)} %pad_add_fusion.5, bf16[2176,2,128,1]{0,2,3,1:T(8,128)(2,1)S(1)} %bitcast.71, bf16[128,2,8,128]{0,3,2,1:T(8,128)(2,1)S(1)} %bitcast.75), kind=kOutput, calls=%fused_computation.29.clone.1 | convolution fusion | flops 1158678656 | bytes 19750912 | tf_op jit(solution)/shard_map/while/body/eval_jaxpr/sub | solution.py:23
  254.4 7.5 %fusion.32 = bf16[2,128,8,128]{3,1,2,0:T(8,128)(2,1)S(1)} fusion(bf16[2176,2,128,1]{0,2,3,1:T(8,128)(2,1)S(1)} %bitcast.70, f32[2,8,128,2176]{2,3,1,0:T(8,128)} %get-tuple-element.147, f32[2,8,128]{2,1,0:T(8,128)S(1)} %get-tuple-element.148), kind=kOutput, calls=%fused_computation.12.clone.1 | convolution fusion | flops 1150025728 | bytes 19472384 | tf_op jit(solution)/shard_map/while/body/eval_jaxpr/kgrl,lkd->rkgd/dot_general | solution.py:25
  262.1 0.8 constant_dynamic-update-slice_fusion.2
  263.0 15.0 %fusion.13 = f32[512,4096]{1,0:T(8,128)} fusion(bf16[512,2048]{1,0:T(8,128)(2,1)} %bitcast.79, bf16[2048,4096]{1,0:T(8,128)(2,1)} %param.15), kind=kOutput, calls=%fused_computation.30 | convolution fusion | flops 8589934592 | bytes 27262976 | tf_op jit(solution)/shard_map/dot_general | solution.py:61
  278.0 150.0 %all-reduce.1 = bf16[512,4096]{1,0:T(8,128)(2,1)} all-reduce(f32[512,4096]{1,0:T(8,128)} %fusion.13), channel_id=1, replica_groups=mesh['seq'=32,'head'=4] {'head'}, use_global_device_ids=true, to_apply=%region_4.5 | all-reduce | flops 2097152 | bytes 12582912 | tf_op jit(solution)/shard_map/psum | solution.py:62
  428.0 2.3 dynamic-slice_convert_fusion
  (62 shorter events, 13.0 us)
Async XLA Ops:
  6.5 78.0 %all-gather.5.cloned.1.call-start = ((), (), s32[]{:S(2)}) async-start(), calls=%async_computation.1 | async-start | bytes 17301504 | tf_op jit(solution)/shard_map/all_gather | solution.py:46
  8.5 137.2 %all-gather.3.cloned.1.call-start = ((), (), s32[]{:S(2)}) async-start(), calls=%async_computation | async-start | bytes 8650752 | tf_op jit(solution)/shard_map/all_gather | solution.py:44
  98.5 47.1 %copy-start = (s32[4]{0:T(128)S(1)}, s32[4]{0:T(128)}, u32[]{:S(2)}) copy-start(s32[4]{0:T(128)} %param.12) | copy-start | bytes 52
  98.5 47.1 %copy-start.1 = (s32[4]{0:T(128)S(1)}, s32[4]{0:T(128)}, u32[]{:S(2)}) copy-start(s32[4]{0:T(128)} %param.14) | copy-start | bytes 52
Sparse Core Ops, SparseCore 0:
  9.7 74.7 all-gather.4
  86.7 58.9 all-gather.2
where the time goes:
time: 438 us; the launch traced here: 437 us
  blocking collectives  150 us (34%)
  waiting for transfers between devices  112 us (26%)
  matrix products  82.5 us (19%)
  local copies, waits for them, and re-layouts  63.9 us (15%)
  between operations  13.4 us (3%)
  other arithmetic  12.3 us (3%)
    psum x1, blocking collectives, body(): summed = lax.psum(partial_value, 'head')  150 us
    all_gather x1, waiting for transfers between devices, body(): everything = lax.all_gather(keys_values, 'seq', axis=0, tiled=True)  73.4 us
    all_gather x1, waiting for transfers between devices, body(): images_all = lax.all_gather(image_kv, 'seq', axis=0, tiled=True)  38.5 us
    sub x4, matrix products, attend(): exponent = jnp.exp(scores - largest)  37.6 us
    dot_general x4, matrix products, attend(): jnp.einsum('kgrl,lkd->rkgd', weights, value_heads, preferred_element_type...  29.9 us
    dynamic_slice x32, local copies, waits for them, and re-layouts, body(): lax.map(one_block, (query_blocks, ancestor_kv, own_blocks, image_of, coun...  22.9 us
    dot_general x1, matrix products, body(): jnp.dot(attended, out_weight, preferred_element_type=jnp.float32)  15 us
    reshape x1, local copies, waits for them, and re-layouts, body(): ancestor_kv = everything.reshape(-1, BS, 2, width_kv)[ancestors]  14 us
  transfers between devices with their start and end apart: 2, of which 2 were waited for; matrix products, arithmetic and copies ran while one was open for 6% of the time, Pallas kernels for 0%

commit v1 on v0

v1 whole, which is shorter than its diff:
```python
import jax
import jax.numpy as jnp
from jax import lax
from jax.experimental import pallas as pl
from jax.experimental.pallas import tpu as pltpu
from jax.sharding import PartitionSpec as P

HEAD_DIM = 128
BS = 128
IMG_TOK = 1024
ANC = 8
SIDE = 4
BLOCKS = 4
SEQ = 32
KVW = 512
HEADS = 16
GROUP = 4
UNITS = HEADS // GROUP
ROWS = GROUP * BS
KEYS = IMG_TOK + ANC * BS + BS
DSHARE = 1024
HALF = 512
BIG = 1e30
SCALE = HEAD_DIM ** (-0.5)
MESH = pl.DeviceIdType.MESH
A_STEPS = (0, -1, 1, 2)


def kernel(
    image_of, ancestors, counts, q_in, kv_in, im_in, w_in, out_ref,
    kv, im, w, q, s_scr, p_scr, v_scr, att, own, stage, zrecv,
    local_sem, kv_send, kv_recv, im_send, im_recv, z_send, z_recv,
):
    me = lax.axis_index("seq")
    z = lax.axis_index("head")
    core = lax.rem(me, 2)
    x = lax.rem(me // 2, SIDE)
    y = me // (2 * SIDE)

    def chip(da, db, c):
        ox = lax.rem(x + da * (1 - c) + db * c + SIDE, SIDE)
        oy = lax.rem(y + da * c + db * (1 - c) + SIDE, SIDE)
        return (oy * SIDE + ox) * 2 + c

    near = [
        (chip(1, 0, core), z), (chip(-1, 0, core), z), (chip(0, 1, core), z), (chip(0, -1, core), z),
        (me + 1 - 2 * core, z),
        (me, lax.rem(z + 1, SIDE)), (me, lax.rem(z + SIDE - 1, SIDE)),
    ]
    a_up, a_down, b_up, b_down, sibling, z_up, z_down = near

    locals_ = [
        pltpu.make_async_copy(kv_in, kv.at[pl.ds(me * BLOCKS, BLOCKS)], local_sem.at[0]),
        pltpu.make_async_copy(im_in, im.at[pl.ds(me * 2, 2)], local_sem.at[1]),
        pltpu.make_async_copy(q_in, q, local_sem.at[2]),
        pltpu.make_async_copy(w_in, w, local_sem.at[3]),
    ]
    for copy in locals_:
        copy.start()

    barrier = pltpu.get_barrier_semaphore()
    for device in near:
        pl.semaphore_signal(barrier, inc=1, device_id=device, device_id_type=MESH)
    pl.semaphore_wait(barrier, len(near))

    class Gather:
        def __init__(self, buf, source, n, send, recv):
            self.buf, self.source, self.n, self.send, self.recv = buf, source, n, send, recv
            self.started = []
            self.siblings = 0

        def rows(self, da, db, part=None, c=None):
            origin = chip(da, db, core if c is None else c)
            if part is None:
                return self.buf.at[pl.ds(origin * self.n, self.n)]
            half = self.n // 2
            return self.buf.at[pl.ds(origin * self.n + part * half, half)]

        def push(self, src, dst, device, index):
            pltpu.make_async_remote_copy(
                src_ref=src, dst_ref=dst, send_sem=self.send.at[index], recv_sem=self.recv.at[index],
                device_id=device, device_id_type=MESH,
            ).start()
            self.started.append((src, index))

        def arrive(self, ref, index):
            pltpu.make_async_copy(ref, ref, self.recv.at[index]).wait()

        def spread(self, da, src=None):
            ref = self.rows(da, 0)
            src = ref if src is None else src
            i = 4 + A_STEPS.index(da) * 4
            self.push(src, ref, b_up, i)
            self.push(src, ref, b_down, i + 1)

        def pair(self, da, db, src=None):
            ref = self.rows(da, db)
            self.push(ref if src is None else src, ref, sibling, 20 + self.siblings)
            self.siblings += 1

        def begin(self):
            ref = self.rows(0, 0)
            self.push(self.source, ref, a_up, 0)
            self.push(self.source, ref, a_down, 1)
            self.spread(0, self.source)
            self.pair(0, 0, self.source)

        def along_a(self):
            self.arrive(self.rows(-1, 0), 0)
            half = self.rows(-1, 0, 0)
            self.push(half, half, a_up, 2)
            self.spread(-1)
            self.pair(-1, 0)
            self.arrive(self.rows(1, 0), 1)
            half = self.rows(1, 0, 1)
            self.push(half, half, a_down, 3)
            self.spread(1)
            self.pair(1, 0)

        def far_a(self):
            self.arrive(self.rows(2, 0, 0), 2)
            self.arrive(self.rows(2, 0, 1), 3)
            self.spread(2)
            self.pair(2, 0)

        def along_b(self, da):
            i = 4 + A_STEPS.index(da) * 4
            self.arrive(self.rows(da, -1), i)
            half = self.rows(da, -1, 0)
            self.push(half, half, b_up, i + 2)
            self.pair(da, -1)
            self.arrive(self.rows(da, 1), i + 1)
            half = self.rows(da, 1, 1)
            self.push(half, half, b_down, i + 3)
            self.pair(da, 1)

        def far_b(self, da):
            i = 4 + A_STEPS.index(da) * 4
            self.arrive(self.rows(da, 2, 0), i + 2)
            self.arrive(self.rows(da, 2, 1), i + 3)
            self.pair(da, 2)

        def finish(self):
            order = [(0, 0), (-1, 0), (1, 0), (0, -1), (0, 1), (2, 0)]
            for da in A_STEPS[1:]:
                order += [(da, -1), (da, 1)]
            order += [(da, 2) for da in A_STEPS]
            for k, (da, db) in enumerate(order):
                self.arrive(self.rows(da, db, c=1 - core), 20 + k)

        def drain(self):
            for src, index in self.started:
                pltpu.make_async_copy(src, src, self.send.at[index]).wait()

    images = Gather(im, im_in, 2, im_send, im_recv)
    blocks = Gather(kv, kv_in, BLOCKS, kv_send, kv_recv)
    images.begin()
    blocks.begin()
    for g in (images, blocks):
        g.along_a()
        g.along_b(0)
        g.far_a()
        for da in A_STEPS[1:]:
            g.along_b(da)
        for da in A_STEPS:
            g.far_b(da)
    for copy in locals_:
        copy.wait()
    images.finish()
    blocks.finish()

    nt = (((1,), (1,)), ((), ()))
    tt = (((0,), (0,)), ((), ()))

    def dot(a, b, dims):
        return lax.dot_general(a, b, dims, preferred_element_type=jnp.float32)

    def attend(b, u):
        j = u // (UNITS // 2)
        k_lanes = pl.ds(pl.multiple_of(j * HEAD_DIM, HEAD_DIM), HEAD_DIM)
        v_lanes = pl.ds(pl.multiple_of(256 + j * HEAD_DIM, HEAD_DIM), HEAD_DIM)
        q_rows = pl.ds(pl.multiple_of(b * BS, BS), BS)
        heads = [
            pl.ds(pl.multiple_of((u * GROUP + h) * HEAD_DIM, HEAD_DIM), HEAD_DIM) for h in range(GROUP)
        ]
        query = jnp.concatenate([q[q_rows, lanes] for lanes in heads], axis=0)
        image = image_of[b]
        live = jnp.full((1, ROWS), counts[b], jnp.int32)

        def image_step(t, top):
            s = dot(im[image * 8 + t, :, k_lanes], query, nt)
            s_scr[pl.ds(pl.multiple_of(t * BS, BS), BS)] = s
            return jnp.maximum(top, jnp.max(s, axis=0, keepdims=True))

        top = lax.fori_loop(0, IMG_TOK // BS, image_step, jnp.full((1, ROWS), -BIG, jnp.float32))

        def ancestor_step(a, top):
            block = ancestors[b, a]
            s = dot(kv[block, :, k_lanes], query, nt)
            s_scr[pl.ds(pl.multiple_of(IMG_TOK + a * BS, BS), BS)] = s
            v_scr[pl.ds(pl.multiple_of(IMG_TOK + a * BS, BS), BS)] = kv[block, :, v_lanes]
            best = jnp.max(s, axis=0, keepdims=True)
            return jnp.maximum(top, jnp.where(live > a, best, -BIG))

        top = lax.fori_loop(0, ANC, ancestor_step, top)

        block = me * BLOCKS + b
        s = dot(kv[block, :, k_lanes], query, nt)
        key_at = lax.broadcasted_iota(jnp.int32, (BS, ROWS), 0)
        token_at = lax.broadcasted_iota(jnp.int32, (BS, ROWS), 1) & (BS - 1)
        s = jnp.where(key_at <= token_at, s, -BIG)
        s_scr[pl.ds(IMG_TOK + ANC * BS, BS)] = s
        v_scr[pl.ds(IMG_TOK + ANC * BS, BS)] = kv[block, :, v_lanes]
        top = jnp.maximum(top, jnp.max(s, axis=0, keepdims=True))

        def weigh(t, total):
            rows = pl.ds(pl.multiple_of(t * BS, BS), BS)
            slot = t - IMG_TOK // BS
            dead = live <= jnp.where(slot < ANC, slot, -1)
            e = jnp.exp((s_scr[rows] - jnp.where(dead, BIG, top)) * SCALE)
            p_scr[rows] = e.astype(jnp.bfloat16)
            return total + jnp.sum(e, axis=0, keepdims=True)

        total = lax.fori_loop(0, KEYS // BS, weigh, jnp.zeros((1, ROWS), jnp.float32))
        for t in range(IMG_TOK // BS):
            v_scr[pl.ds(t * BS, BS)] = im[image * 8 + t, :, v_lanes]
        o = dot(v_scr[...], p_scr[...], tt)
        o = o / total
        for h, lanes in enumerate(heads):
            att[:, lanes] = o[:, h * BS : (h + 1) * BS].T.astype(jnp.bfloat16)

    def project(d, half):
        cols = pl.ds(pl.multiple_of(d * DSHARE + half * HALF, HALF), HALF)
        return dot(att[...], w[:, cols], (((1,), (0,)), ((), ())))

    far, up, down = lax.rem(z + 2, SIDE), lax.rem(z + 1, SIDE), lax.rem(z + 3, SIDE)

    def z_copy(b, slot, device):
        return pltpu.make_async_remote_copy(
            src_ref=stage.at[b, slot], dst_ref=zrecv.at[b, slot],
            send_sem=z_send.at[b, slot], recv_sem=z_recv.at[b, slot],
            device_id=device, device_id_type=MESH,
        )

    def z_wait(b, slot):
        pltpu.make_async_copy(zrecv.at[b, slot], zrecv.at[b, slot], z_recv.at[b, slot]).wait()

    def one_block(b, carry):
        def unit(u, carry):
            attend(b, u)
            return carry

        lax.fori_loop(0, UNITS, unit, 0)
        for slot, d, half, device in ((0, far, 0, z_up), (1, far, 1, z_down), (2, up, 1, z_up), (3, down, 0, z_down)):
            stage[b, slot] = project(d, half).astype(jnp.bfloat16)
            z_copy(b, slot, device).start()
        for half in range(2):
            own[pl.ds(pl.multiple_of(b * BS, BS), BS), half * HALF : (half + 1) * HALF] = project(z, half)
        for slot, arrived, d, half, device in ((4, 0, up, 0, z_up), (5, 1, down, 1, z_down)):
            part = project(d, half)
            z_wait(b, arrived)
            stage[b, slot] = (part + zrecv[b, arrived].astype(jnp.float32)).astype(jnp.bfloat16)
            z_copy(b, slot, device).start()
        return carry

    lax.fori_loop(0, BLOCKS, one_block, 0)

    def last(b, carry):
        rows = pl.ds(pl.multiple_of(b * BS, BS), BS)
        for slot in (2, 3, 4, 5):
            z_wait(b, slot)
        for half, (one, two) in enumerate(((3, 4), (2, 5))):
            cols = slice(half * HALF, (half + 1) * HALF)
            total = own[rows, cols] + zrecv[b, one].astype(jnp.float32) + zrecv[b, two].astype(jnp.float32)
            out_ref[rows, cols] = total.astype(jnp.bfloat16)
        for slot in range(6):
            pltpu.make_async_copy(stage.at[b, slot], stage.at[b, slot], z_send.at[b, slot]).wait()
        return carry

    lax.fori_loop(0, BLOCKS, last, 0)
    images.drain()
    blocks.drain()


def body(queries, keys_values, image_kv, image_of, ancestors, counts, out_weight):
    kv = keys_values.reshape(BLOCKS, BS, KVW)
    im = image_kv.reshape(2, BS, KVW)
    smem = pl.BlockSpec(memory_space=pltpu.SMEM)
    hbm = pl.BlockSpec(memory_space=pl.ANY)
    bf16, f32 = jnp.bfloat16, jnp.float32
    return pl.pallas_call(
        kernel,
        out_shape=jax.ShapeDtypeStruct((BLOCKS * BS, DSHARE), bf16),
        in_specs=[smem] * 3 + [hbm] * 4,
        out_specs=pl.BlockSpec(memory_space=pltpu.VMEM),
        scratch_shapes=[
            pltpu.VMEM((SEQ * BLOCKS, BS, KVW), bf16),
            pltpu.VMEM((SEQ * 2, BS, KVW), bf16),
            pltpu.VMEM(out_weight.shape, bf16),
            pltpu.VMEM(queries.shape, bf16),
            pltpu.VMEM((KEYS, ROWS), f32),
            pltpu.VMEM((KEYS, ROWS), bf16),
            pltpu.VMEM((KEYS, HEAD_DIM), bf16),
            pltpu.VMEM((BS, HEADS * HEAD_DIM), bf16),
            pltpu.VMEM((BLOCKS * BS, DSHARE), f32),
            pltpu.VMEM((BLOCKS, 6, BS, HALF), bf16),
            pltpu.VMEM((BLOCKS, 6, BS, HALF), bf16),
            pltpu.SemaphoreType.DMA((4,)),
            pltpu.SemaphoreType.DMA((36,)),
            pltpu.SemaphoreType.DMA((36,)),
            pltpu.SemaphoreType.DMA((36,)),
            pltpu.SemaphoreType.DMA((36,)),
            pltpu.SemaphoreType.DMA((BLOCKS, 6)),
            pltpu.SemaphoreType.DMA((BLOCKS, 6)),
        ],
        compiler_params=pltpu.CompilerParams(
            collective_id=0, has_side_effects=True, vmem_limit_bytes=62 * 1024 * 1024
        ),
        name="tree_attention",
    )(image_of, ancestors, counts, queries, kv, im, out_weight)


def solution(mesh):
    in_specs = (
        P("seq", "head"),
        P("seq", None, "head"),
        P("seq", None, "head"),
        P("seq"),
        P("seq", None),
        P("seq"),
        P("head", None),
    )
    out_specs = P("seq", "head")
    return jax.shard_map(body, mesh=mesh, in_specs=in_specs, out_specs=out_specs, check_vma=False)
```

time: 438 us -> 199 us (0.45)
  Pallas kernels: 0 us -> 193 us
  blocking collectives: 150 us -> 0 us
  waiting for transfers between devices: 112 us -> 0 us
  matrix products: 82.5 us -> 0 us
  local copies, waits for them, and re-layouts: 63.9 us -> 6.26 us
  between operations: 13.4 us -> 0.01 us
  other arithmetic: 12.3 us -> 0 us
    pallas_call x0 -> x1, Pallas kernels: none -> 193 us  [body(): pl.pallas_call(kernel, out_shape=jax.ShapeDtypeStruct((BLOCKS * BS, DSHAR...]
    psum x1 -> x0, blocking collectives: 150 us -> none  [body(): summed = lax.psum(partial_value, 'head')]
    all_gather x2 -> x0, waiting for transfers between devices: 112 us -> none  [the longest x1 73.4 us: body(): everything = lax.all_gather(keys_values, 'seq', axis=0, tiled=True)]
    dot_general x5 -> x0, matrix products: 44.9 us -> none  [the longest x4 29.9 us: attend(): jnp.einsum('kgrl,lkd->rkgd', weights, value_heads, preferred_element_type...]
    sub x4 -> x0, matrix products: 37.6 us -> none  [attend(): exponent = jnp.exp(scores - largest)]
    dynamic_slice x36 -> x0, local copies, waits for them, and re-layouts: 28.1 us -> none  [the longest x32 22.9 us: body(): lax.map(one_block, (query_blocks, ancestor_kv, own_blocks, image_of, coun...]
    reshape x5 -> x2, local copies, waits for them, and re-layouts: 16 us -> 4 us  [the longest x1 2.17 us: body(): kv = keys_values.reshape(BLOCKS, BS, KVW)]
    concatenate x12 -> x0, other arithmetic: 8.95 us -> none  [the longest x8 8.28 us: allowed_mask(): return jnp.concatenate([image_part, ancestor_part, own_part], axis=1)]
  transfers between devices with their start and end apart: 2 -> 0, of which waited for: 2 -> 0; matrix products, arithmetic and copies ran while one was open for 6% -> 0% of each run, Pallas kernels for 0% -> 0%
where the time goes in v1:
time: 199 us
  Pallas kernels  193 us (97%)
  local copies, waits for them, and re-layouts  6.26 us (3%)
    pallas_call x1, Pallas kernels, body(): pl.pallas_call(kernel, out_shape=jax.ShapeDtypeStruct((BLOCKS * BS, DSHAR...  193 us

profile of v1, /device:TPU:0, one launch (start us, length us, event | category | flops | bytes accessed | tf_op | source)
XLA Modules:
  0.0 199.2 jit_solution(3920947926612943074)
XLA Ops:
  0.0 1.8 reshape.7.im_in
  1.8 2.2 %reshape.6.kv_in = bf16[4,128,512]{2,1,0:T(8,128)(2,1)} reshape(bf16[512,2,256]{2,1,0:T(2,128)(2,1)} %param.8) | data formatting | bytes 1048576 | tf_op jit(solution)/shard_map/reshape | solution.py:286
  4.0 193.0 %tree_attention.1 = bf16[512,1024]{1,0:T(8,128)(2,1)} custom-call(s32[4]{0:T(128)} %image_of.1, s32[4,8]{1,0:T(4,128)} %ancestors.1, s32[4]{0:T(128)} %counts.1, bf16[512,2048]{1,0:T(8,128)(2,1)} %q_in.1, bf16[4,128,512]{2,1,0:T(8,128)(2,1)} %reshape.6.kv_in, bf16[2,128,512]{2,1,0:T(8,128)(2,1)} %reshape.7.im_in, bf16[2048,4096]{1,0:T(8,128)(2,1)} %w_in.1), custom_call_target="tpu_custom_call" | custom-call | tf_op jit(solution)/shard_map/tree_attention/pallas_call | solution.py:291
  197.0 2.3 %copy.9 = bf16[512,1024]{1,0:T(8,128)(2,1)} copy(bf16[512,1024]{1,0:T(8,128)(2,1)} %tree_attention.1) | data formatting | bytes 2097152

commit v2 on v1

--- a/solution.py
+++ b/solution.py
@@ -1,3 +1,5 @@
+import math
+
 import jax
 import jax.numpy as jnp
 from jax import lax
@@ -17,18 +19,18 @@
 GROUP = 4
 UNITS = HEADS // GROUP
 ROWS = GROUP * BS
-KEYS = IMG_TOK + ANC * BS + BS
 DSHARE = 1024
 HALF = 512
 BIG = 1e30
-SCALE = HEAD_DIM ** (-0.5)
+SCALE2 = HEAD_DIM ** (-0.5) * math.log2(math.e)
 MESH = pl.DeviceIdType.MESH
 A_STEPS = (0, -1, 1, 2)
+HALVES = (2, 3, 6, 7, 10, 11, 14, 15, 18, 19)
 
 
 def kernel(
     image_of, ancestors, counts, q_in, kv_in, im_in, w_in, out_ref,
-    kv, im, w, q, s_scr, p_scr, v_scr, att, own, stage, zrecv,
+    kv, im, w, q, acc, stat, att, own, stage, zrecv,
     local_sem, kv_send, kv_recv, im_send, im_recv, z_send, z_recv,
 ):
     me = lax.axis_index("seq")
@@ -81,7 +83,7 @@
                 src_ref=src, dst_ref=dst, send_sem=self.send.at[index], recv_sem=self.recv.at[index],
                 device_id=device, device_id_type=MESH,
             ).start()
-            self.started.append((src, index))
+            self.started.append(index)
 
         def arrive(self, ref, index):
             pltpu.make_async_copy(ref, ref, self.recv.at[index]).wait()
@@ -149,89 +151,97 @@
                 self.arrive(self.rows(da, db, c=1 - core), 20 + k)
 
         def drain(self):
-            for src, index in self.started:
-                pltpu.make_async_copy(src, src, self.send.at[index]).wait()
+            for index in self.started:
+                part = self.n // 2 if index in HALVES else self.n
+                ref = self.buf.at[pl.ds(0, part)]
+                pltpu.make_async_copy(ref, ref, self.send.at[index]).wait()
 
     images = Gather(im, im_in, 2, im_send, im_recv)
     blocks = Gather(kv, kv_in, BLOCKS, kv_send, kv_recv)
     images.begin()
+    images.along_a()
     blocks.begin()
-    for g in (images, blocks):
-        g.along_a()
-        g.along_b(0)
-        g.far_a()
-        for da in A_STEPS[1:]:
-            g.along_b(da)
-        for da in A_STEPS:
-            g.far_b(da)
-    for copy in locals_:
+    images.along_b(0)
+    images.far_a()
+    for da in A_STEPS[1:]:
+        images.along_b(da)
+    for da in A_STEPS:
+        images.far_b(da)
+    for copy in locals_[:3]:
         copy.wait()
     images.finish()
-    blocks.finish()
 
     nt = (((1,), (1,)), ((), ()))
-    tt = (((0,), (0,)), ((), ()))
+    nn = (((1,), (0,)), ((), ()))
 
     def dot(a, b, dims):
         return lax.dot_general(a, b, dims, preferred_element_type=jnp.float32)
 
-    def attend(b, u):
-        j = u // (UNITS // 2)
-        k_lanes = pl.ds(pl.multiple_of(j * HEAD_DIM, HEAD_DIM), HEAD_DIM)
-        v_lanes = pl.ds(pl.multiple_of(256 + j * HEAD_DIM, HEAD_DIM), HEAD_DIM)
-        q_rows = pl.ds(pl.multiple_of(b * BS, BS), BS)
-        heads = [
+    def queries_of(b, u):
+        rows = pl.ds(pl.multiple_of(b * BS, BS), BS)
+        lanes = [
             pl.ds(pl.multiple_of((u * GROUP + h) * HEAD_DIM, HEAD_DIM), HEAD_DIM) for h in range(GROUP)
         ]
-        query = jnp.concatenate([q[q_rows, lanes] for lanes in heads], axis=0)
+        return jnp.concatenate([q[rows, cols] for cols in lanes], axis=0)
+
+    def lanes_of(j):
+        return (
+            pl.ds(pl.multiple_of(j * HEAD_DIM, HEAD_DIM), HEAD_DIM),
+            pl.ds(pl.multiple_of(256 + j * HEAD_DIM, HEAD_DIM), HEAD_DIM),
+        )
+
+    def image_part(b, j):
+        k_lanes, v_lanes = lanes_of(j)
         image = image_of[b]
+        tiles = range(IMG_TOK // BS)
+        k = jnp.concatenate([im[image * 8 + t, :, k_lanes] for t in tiles], axis=0)
+        v = jnp.concatenate([im[image * 8 + t, :, v_lanes] for t in tiles], axis=0).T
+        for r in range(2):
+            u = 2 * j + r
+            s = dot(k, queries_of(b, u), nt)
+            top = jnp.max(s, axis=0, keepdims=True)
+            e = jnp.exp2((s - top) * SCALE2)
+            slot = b * UNITS + u
+            stat[slot, 0:1] = top
+            stat[slot, 1:2] = jnp.sum(e, axis=0, keepdims=True)
+            acc[slot] = dot(v, e.astype(jnp.bfloat16), nn)
+
+    def rest_part(b, j):
+        k_lanes, v_lanes = lanes_of(j)
         live = jnp.full((1, ROWS), counts[b], jnp.int32)
-
-        def image_step(t, top):
-            s = dot(im[image * 8 + t, :, k_lanes], query, nt)
-            s_scr[pl.ds(pl.multiple_of(t * BS, BS), BS)] = s
-            return jnp.maximum(top, jnp.max(s, axis=0, keepdims=True))
-
-        top = lax.fori_loop(0, IMG_TOK // BS, image_step, jnp.full((1, ROWS), -BIG, jnp.float32))
-
-        def ancestor_step(a, top):
-            block = ancestors[b, a]
-            s = dot(kv[block, :, k_lanes], query, nt)
-            s_scr[pl.ds(pl.multiple_of(IMG_TOK + a * BS, BS), BS)] = s
-            v_scr[pl.ds(pl.multiple_of(IMG_TOK + a * BS, BS), BS)] = kv[block, :, v_lanes]
-            best = jnp.max(s, axis=0, keepdims=True)
-            return jnp.maximum(top, jnp.where(live > a, best, -BIG))
-
-        top = lax.fori_loop(0, ANC, ancestor_step, top)
-
-        block = me * BLOCKS + b
-        s = dot(kv[block, :, k_lanes], query, nt)
+        at = [ancestors[b, a] for a in range(ANC)] + [me * BLOCKS + b]
+        k = jnp.concatenate([kv[i, :, k_lanes] for i in at], axis=0)
+        v = jnp.concatenate([kv[i, :, v_lanes] for i in at], axis=0).T
         key_at = lax.broadcasted_iota(jnp.int32, (BS, ROWS), 0)
         token_at = lax.broadcasted_iota(jnp.int32, (BS, ROWS), 1) & (BS - 1)
-        s = jnp.where(key_at <= token_at, s, -BIG)
-        s_scr[pl.ds(IMG_TOK + ANC * BS, BS)] = s
-        v_scr[pl.ds(IMG_TOK + ANC * BS, BS)] = kv[block, :, v_lanes]
-        top = jnp.maximum(top, jnp.max(s, axis=0, keepdims=True))
-
-        def weigh(t, total):
-            rows = pl.ds(pl.multiple_of(t * BS, BS), BS)
-            slot = t - IMG_TOK // BS
-            dead = live <= jnp.where(slot < ANC, slot, -1)
-            e = jnp.exp((s_scr[rows] - jnp.where(dead, BIG, top)) * SCALE)
-            p_scr[rows] = e.astype(jnp.bfloat16)
-            return total + jnp.sum(e, axis=0, keepdims=True)
-
-        total = lax.fori_loop(0, KEYS // BS, weigh, jnp.zeros((1, ROWS), jnp.float32))
-        for t in range(IMG_TOK // BS):
-            v_scr[pl.ds(t * BS, BS)] = im[image * 8 + t, :, v_lanes]
-        o = dot(v_scr[...], p_scr[...], tt)
-        o = o / total
-        for h, lanes in enumerate(heads):
-            att[:, lanes] = o[:, h * BS : (h + 1) * BS].T.astype(jnp.bfloat16)
+        for r in range(2):
+            u = 2 * j + r
+            slot = b * UNITS + u
+            s = dot(k, queries_of(b, u), nt)
+            parts = [s[a * BS : (a + 1) * BS] for a in range(ANC + 1)]
+            parts[ANC] = jnp.where(key_at <= token_at, parts[ANC], -BIG)
+            before = stat[slot, 0:1]
+            top = jnp.maximum(before, jnp.max(parts[ANC], axis=0, keepdims=True))
+            for a in range(ANC):
+                best = jnp.max(parts[a], axis=0, keepdims=True)
+                top = jnp.maximum(top, jnp.where(live > a, best, -BIG))
+            keep = jnp.exp2((before - top) * SCALE2)
+            total = stat[slot, 1:2] * keep
+            weights = []
+            for a in range(ANC + 1):
+                under = jnp.where(live > a, top, BIG) if a < ANC else top
+                e = jnp.exp2((parts[a] - under) * SCALE2)
+                total = total + jnp.sum(e, axis=0, keepdims=True)
+                weights.append(e.astype(jnp.bfloat16))
+            o = acc[slot] * keep + dot(v, jnp.concatenate(weights, axis=0), nn)
+            o = o / total
+            for h in range(GROUP):
+                cols = pl.ds(pl.multiple_of((u * GROUP + h) * HEAD_DIM, HEAD_DIM), HEAD_DIM)
+                att[:, cols] = o[:, h * BS : (h + 1) * BS].T.astype(jnp.bfloat16)
 
     def project(d, half):
         cols = pl.ds(pl.multiple_of(d * DSHARE + half * HALF, HALF), HALF)
-        return dot(att[...], w[:, cols], (((1,), (0,)), ((), ())))
+        return dot(att[...], w[:, cols], nn)
 
     far, up, down = lax.rem(z + 2, SIDE), lax.rem(z + 1, SIDE), lax.rem(z + 3, SIDE)
 
@@ -246,11 +256,11 @@
         pltpu.make_async_copy(zrecv.at[b, slot], zrecv.at[b, slot], z_recv.at[b, slot]).wait()
 
     def one_block(b, carry):
-        def unit(u, carry):
-            attend(b, u)
+        def heads(j, carry):
+            rest_part(b, j)
             return carry
 
-        lax.fori_loop(0, UNITS, unit, 0)
+        lax.fori_loop(0, 2, heads, 0)
         for slot, d, half, device in ((0, far, 0, z_up), (1, far, 1, z_down), (2, up, 1, z_up), (3, down, 0, z_down)):
             stage[b, slot] = project(d, half).astype(jnp.bfloat16)
             z_copy(b, slot, device).start()
@@ -263,6 +273,22 @@
             z_copy(b, slot, device).start()
         return carry
 
+    events = [
+        blocks.along_a, lambda: blocks.along_b(0), blocks.far_a,
+        lambda: blocks.along_b(-1), lambda: blocks.along_b(1), lambda: blocks.along_b(2),
+    ]
+
+    def image_step(i, carry):
+        for k, event in enumerate(events):
+            pl.when(i == k)(event)
+        image_part(i // 2, lax.rem(i, 2))
+        return carry
+
+    lax.fori_loop(0, 2 * BLOCKS, image_step, 0)
+    for da in A_STEPS:
+        blocks.far_b(da)
+    locals_[3].wait()
+    blocks.finish()
     lax.fori_loop(0, BLOCKS, one_block, 0)
 
     def last(b, carry):
@@ -298,9 +324,8 @@
             pltpu.VMEM((SEQ * 2, BS, KVW), bf16),
             pltpu.VMEM(out_weight.shape, bf16),
             pltpu.VMEM(queries.shape, bf16),
-            pltpu.VMEM((KEYS, ROWS), f32),
-            pltpu.VMEM((KEYS, ROWS), bf16),
-            pltpu.VMEM((KEYS, HEAD_DIM), bf16),
+            pltpu.VMEM((BLOCKS * UNITS, HEAD_DIM, ROWS), f32),
+            pltpu.VMEM((BLOCKS * UNITS, 8, ROWS), f32),
             pltpu.VMEM((BS, HEADS * HEAD_DIM), bf16),
             pltpu.VMEM((BLOCKS * BS, DSHARE), f32),
             pltpu.VMEM((BLOCKS, 6, BS, HALF), bf16),

time: 199 us -> 139 us (0.70)
  Pallas kernels: 193 us -> 132 us
    pallas_call x1, Pallas kernels: 193 us -> 132 us  [body(): pl.pallas_call(kernel, out_shape=jax.ShapeDtypeStruct((BLOCKS * BS, DSHAR...]
where the time goes in v2:
time: 139 us
  Pallas kernels  132 us (95%)
  local copies, waits for them, and re-layouts  6.26 us (5%)
    pallas_call x1, Pallas kernels, body(): pl.pallas_call(kernel, out_shape=jax.ShapeDtypeStruct((BLOCKS * BS, DSHAR...  132 us

profile of v2, /device:TPU:0, one launch (start us, length us, event | category | flops | bytes accessed | tf_op | source)
XLA Modules:
  0.0 138.7 jit_solution(9387051513726330581)
XLA Ops:
  0.0 1.8 %reshape.7.im_in = bf16[2,128,512]{2,1,0:T(8,128)(2,1)} reshape(bf16[256,2,256]{2,1,0:T(2,128)(2,1)} %param.9) | data formatting | bytes 524288 | tf_op jit(solution)/shard_map/reshape | solution.py:313
  1.8 2.2 %reshape.6.kv_in = bf16[4,128,512]{2,1,0:T(8,128)(2,1)} reshape(bf16[512,2,256]{2,1,0:T(2,128)(2,1)} %param.8) | data formatting | bytes 1048576 | tf_op jit(solution)/shard_map/reshape | solution.py:312
  4.0 132.5 %tree_attention.1 = bf16[512,1024]{1,0:T(8,128)(2,1)} custom-call(s32[4]{0:T(128)} %image_of.1, s32[4,8]{1,0:T(4,128)} %ancestors.1, s32[4]{0:T(128)} %counts.1, bf16[512,2048]{1,0:T(8,128)(2,1)} %q_in.1, bf16[4,128,512]{2,1,0:T(8,128)(2,1)} %reshape.6.kv_in, bf16[2,128,512]{2,1,0:T(8,128)(2,1)} %reshape.7.im_in, bf16[2048,4096]{1,0:T(8,128)(2,1)} %w_in.1), custom_call_target="tpu_custom_call" | custom-call | tf_op jit(solution)/shard_map/tree_attention/pallas_call | solution.py:317
  136.5 2.3 %copy.9 = bf16[512,1024]{1,0:T(8,128)(2,1)} copy(bf16[512,1024]{1,0:T(8,128)(2,1)} %tree_attention.1) | data formatting | bytes 2097152

commit v3 on v2

--- a/solution.py
+++ b/solution.py
@@ -30,8 +30,10 @@
 
 def kernel(
     image_of, ancestors, counts, q_in, kv_in, im_in, w_in, out_ref,
-    kv, im, w, q, acc, stat, att, own, stage, zrecv,
-    local_sem, kv_send, kv_recv, im_send, im_recv, z_send, z_recv,
+    im, w, q, acc, stat, att, hold, own, stage, zrecv,
+    row_own, row_prev, row_next, row_far, picked, passing, got, table, needs,
+    local_sem, im_send, im_recv, row_send, row_recv, pass_send, pass_recv, got_send, got_recv,
+    table_send, table_recv, z_send, z_recv,
 ):
     me = lax.axis_index("seq")
     z = lax.axis_index("head")
@@ -44,15 +46,19 @@
         oy = lax.rem(y + da * c + db * (1 - c) + SIDE, SIDE)
         return (oy * SIDE + ox) * 2 + c
 
-    near = [
-        (chip(1, 0, core), z), (chip(-1, 0, core), z), (chip(0, 1, core), z), (chip(0, -1, core), z),
-        (me + 1 - 2 * core, z),
-        (me, lax.rem(z + 1, SIDE)), (me, lax.rem(z + SIDE - 1, SIDE)),
-    ]
-    a_up, a_down, b_up, b_down, sibling, z_up, z_down = near
+    def other(device):
+        return device + 1 - 2 * core
+
+    a_up, a_down = (chip(1, 0, core), z), (chip(-1, 0, core), z)
+    b_up, b_down = (chip(0, 1, core), z), (chip(0, -1, core), z)
+    sibling = (other(me), z)
+    z_up, z_down = (me, lax.rem(z + 1, SIDE)), (me, lax.rem(z + SIDE - 1, SIDE))
+    near = [sibling, z_up, z_down]
+    for da, db in ((1, 0), (-1, 0), (2, 0), (0, 1), (0, -1), (0, 2)):
+        near += [(chip(da, db, 0), z), (chip(da, db, 1), z)]
 
     locals_ = [
-        pltpu.make_async_copy(kv_in, kv.at[pl.ds(me * BLOCKS, BLOCKS)], local_sem.at[0]),
+        pltpu.make_async_copy(kv_in, row_own, local_sem.at[0]),
         pltpu.make_async_copy(im_in, im.at[pl.ds(me * 2, 2)], local_sem.at[1]),
         pltpu.make_async_copy(q_in, q, local_sem.at[2]),
         pltpu.make_async_copy(w_in, w, local_sem.at[3]),
@@ -63,7 +69,29 @@
     barrier = pltpu.get_barrier_semaphore()
     for device in near:
         pl.semaphore_signal(barrier, inc=1, device_id=device, device_id_type=MESH)
+
+    lane = lax.broadcasted_iota(jnp.int32, (8, 128), 1)
+    listed = jnp.zeros((8, 128), jnp.int32)
+    for b in range(BLOCKS):
+        for a in range(ANC):
+            block = jnp.full((8, 128), ancestors[b, a], jnp.int32)
+            listed = jnp.maximum(listed, jnp.where((block >> 2) == lane, block & 3, 0))
+    table[0, 0] = listed
+
     pl.semaphore_wait(barrier, len(near))
+
+    def copy_to(src, dst, send, recv, device):
+        return pltpu.make_async_remote_copy(
+            src_ref=src, dst_ref=dst, send_sem=send, recv_sem=recv, device_id=device, device_id_type=MESH,
+        )
+
+    def wait_for(ref, sem):
+        pltpu.make_async_copy(ref, ref, sem).wait()
+
+    table_slots = [(k, r) for k in range(SIDE) for r in range(2) if (k, r) != (0, 0)]
+    for k, r in table_slots:
+        device = (chip(0, -k, core if r == 0 else 1 - core), z)
+        copy_to(table.at[0, 0], table.at[k, r], table_send.at[k, r], table_recv.at[k, r], device).start()
 
     class Gather:
         def __init__(self, buf, source, n, send, recv):
@@ -157,17 +185,82 @@
                 pltpu.make_async_copy(ref, ref, self.send.at[index]).wait()
 
     images = Gather(im, im_in, 2, im_send, im_recv)
-    blocks = Gather(kv, kv_in, BLOCKS, kv_send, kv_recv)
+    low, high = pl.ds(0, 2), pl.ds(2, 2)
+    row_copies = [
+        copy_to(kv_in.at[low], row_prev.at[low], row_send.at[0], row_recv.at[0], a_up),
+        copy_to(kv_in.at[high], row_next.at[high], row_send.at[1], row_recv.at[1], a_down),
+        copy_to(kv_in.at[high], row_prev.at[high], row_send.at[2], row_recv.at[2], a_up),
+        copy_to(kv_in.at[low], row_next.at[low], row_send.at[3], row_recv.at[3], a_down),
+        copy_to(row_prev.at[low], row_far.at[low], row_send.at[4], row_recv.at[4], a_up),
+        copy_to(row_next.at[high], row_far.at[high], row_send.at[5], row_recv.at[5], a_down),
+    ]
+
+    def row_begin():
+        for copy in row_copies[:4]:
+            copy.start()
+
+    def row_pass():
+        row_copies[0].wait_recv()
+        row_copies[4].start()
+        row_copies[1].wait_recv()
+        row_copies[5].start()
+
+    SIDES = (0, -1, 1, 2)
+
+    def origin(r, k, i):
+        return chip(A_STEPS[i], SIDES[k], core if r == 0 else 1 - core)
+
+    def deliver(src, r, k, i, source, device):
+        if r == 1:
+            device = (other(device[0]), z)
+        return copy_to(src, got.at[source], got_send.at[r, k, i], got_recv.at[r, k, i], device)
+
+    def pass_copy(r, i):
+        device = b_up if i < 2 else b_down
+        return copy_to(picked.at[2, r, i], passing.at[r, i], pass_send.at[r, i], pass_recv.at[r, i], device)
+
+    def hand_on(r, i):
+        device, back = (b_up, -1) if i < 2 else (b_down, 1)
+        return deliver(passing.at[r, i], r, 3, i, chip(A_STEPS[i], back, core), device)
+
+    def pick(i, row):
+        source = chip(A_STEPS[i], 0, core)
+        for r in range(2):
+            picked[2, r, i] = row[needs[2, r, 0, source]]
+            pass_copy(r, i).start()
+        for n, (k, slot, device) in enumerate(((1, 1, b_up), (2, 3, b_down))):
+            for r in range(2):
+                picked[n, r, i] = row[needs[slot, r, 0, source]]
+                deliver(picked.at[n, r, i], r, k, i, source, device).start()
+        picked[3, 1, i] = row[needs[0, 1, 0, source]]
+        deliver(picked.at[3, 1, i], 1, 0, i, source, (me, z)).start()
+        got[source] = row[needs[0, 0, 0, source]]
+
     images.begin()
+    row_begin()
     images.along_a()
-    blocks.begin()
+    for k, r in table_slots:
+        wait_for(table.at[k, r], table_recv.at[k, r])
+    to_scalars = pltpu.make_async_copy(table, needs, local_sem.at[4])
+    to_scalars.start()
     images.along_b(0)
     images.far_a()
+    to_scalars.wait()
+    locals_[0].wait()
+    pick(0, row_own)
+    row_pass()
     for da in A_STEPS[1:]:
         images.along_b(da)
+    row_copies[2].wait_recv()
+    pick(1, row_prev)
+    row_copies[3].wait_recv()
+    pick(2, row_next)
     for da in A_STEPS:
         images.far_b(da)
-    for copy in locals_[:3]:
+    row_copies[4].wait_recv()
+    row_copies[5].wait_recv()
+    pick(3, row_far)
+    for copy in locals_[1:3]:
         copy.wait()
     images.finish()
 
@@ -190,46 +283,53 @@
             pl.ds(pl.multiple_of(256 + j * HEAD_DIM, HEAD_DIM), HEAD_DIM),
         )
 
+    key_at = lax.broadcasted_iota(jnp.int32, (BS, ROWS), 0)
+    token_at = lax.broadcasted_iota(jnp.int32, (BS, ROWS), 1) & (BS - 1)
+
     def image_part(b, j):
-        k_lanes, v_lanes = lanes_of(j)
+        lanes = lanes_of(j)
         image = image_of[b]
-        tiles = range(IMG_TOK // BS)
-        k = jnp.concatenate([im[image * 8 + t, :, k_lanes] for t in tiles], axis=0)
-        v = jnp.concatenate([im[image * 8 + t, :, v_lanes] for t in tiles], axis=0).T
-        for r in range(2):
-            u = 2 * j + r
-            s = dot(k, queries_of(b, u), nt)
-            top = jnp.max(s, axis=0, keepdims=True)
-            e = jnp.exp2((s - top) * SCALE2)
-            slot = b * UNITS + u
-            stat[slot, 0:1] = top
-            stat[slot, 1:2] = jnp.sum(e, axis=0, keepdims=True)
-            acc[slot] = dot(v, e.astype(jnp.bfloat16), nn)
-
-    def rest_part(b, j):
-        k_lanes, v_lanes = lanes_of(j)
-        live = jnp.full((1, ROWS), counts[b], jnp.int32)
-        at = [ancestors[b, a] for a in range(ANC)] + [me * BLOCKS + b]
-        k = jnp.concatenate([kv[i, :, k_lanes] for i in at], axis=0)
-        v = jnp.concatenate([kv[i, :, v_lanes] for i in at], axis=0).T
-        key_at = lax.broadcasted_iota(jnp.int32, (BS, ROWS), 0)
-        token_at = lax.broadcasted_iota(jnp.int32, (BS, ROWS), 1) & (BS - 1)
+        k, v = (
+            jnp.concatenate(
+                [im[image * 8 + t, :, cols] for t in range(IMG_TOK // BS)] + [row_own[b, :, cols]], axis=0
+            )
+            for cols in lanes
+        )
+        v = v.T
         for r in range(2):
             u = 2 * j + r
             slot = b * UNITS + u
             s = dot(k, queries_of(b, u), nt)
-            parts = [s[a * BS : (a + 1) * BS] for a in range(ANC + 1)]
-            parts[ANC] = jnp.where(key_at <= token_at, parts[ANC], -BIG)
+            s, s_own = s[:IMG_TOK], s[IMG_TOK:]
+            s_own = jnp.where(key_at <= token_at, s_own, -BIG)
+            top = jnp.maximum(jnp.max(s, axis=0, keepdims=True), jnp.max(s_own, axis=0, keepdims=True))
+            e = jnp.exp2((s - top) * SCALE2)
+            e_own = jnp.exp2((s_own - top) * SCALE2)
+            stat[slot, 0:1] = top
+            stat[slot, 1:2] = jnp.sum(e, axis=0, keepdims=True) + jnp.sum(e_own, axis=0, keepdims=True)
+            acc[slot] = dot(v, jnp.concatenate([e.astype(jnp.bfloat16), e_own.astype(jnp.bfloat16)], axis=0), nn)
+
+    def rest_part(b, j):
+        k_lanes, v_lanes = lanes_of(j)
+        live = jnp.full((1, ROWS), counts[b], jnp.int32)
+        at = [lax.shift_right_logical(ancestors[b, a], 2) for a in range(ANC)]
+        k = jnp.concatenate([got[i, :, k_lanes] for i in at], axis=0)
+        v = jnp.concatenate([got[i, :, v_lanes] for i in at], axis=0).T
+        for r in range(2):
+            u = 2 * j + r
+            slot = b * UNITS + u
+            s = dot(k, queries_of(b, u), nt)
+            parts = [s[a * BS : (a + 1) * BS] for a in range(ANC)]
             before = stat[slot, 0:1]
-            top = jnp.maximum(before, jnp.max(parts[ANC], axis=0, keepdims=True))
+            top = before
             for a in range(ANC):
                 best = jnp.max(parts[a], axis=0, keepdims=True)
                 top = jnp.maximum(top, jnp.where(live > a, best, -BIG))
             keep = jnp.exp2((before - top) * SCALE2)
             total = stat[slot, 1:2] * keep
             weights = []
-            for a in range(ANC + 1):
-                under = jnp.where(live > a, top, BIG) if a < ANC else top
+            for a in range(ANC):
+                under = jnp.where(live > a, top, BIG)
                 e = jnp.exp2((parts[a] - under) * SCALE2)
                 total = total + jnp.sum(e, axis=0, keepdims=True)
                 weights.append(e.astype(jnp.bfloat16))
@@ -253,7 +353,13 @@
         )
 
     def z_wait(b, slot):
-        pltpu.make_async_copy(zrecv.at[b, slot], zrecv.at[b, slot], z_recv.at[b, slot]).wait()
+        wait_for(zrecv.at[b, slot], z_recv.at[b, slot])
+
+    def pass_on(b):
+        for k, (slot, device) in enumerate(((4, z_up), (5, z_down))):
+            z_wait(b, k)
+            stage[b, slot] = (hold[k] + zrecv[b, k].astype(jnp.float32)).astype(jnp.bfloat16)
+            z_copy(b, slot, device).start()
 
     def one_block(b, carry):
         def heads(j, carry):
@@ -261,35 +367,40 @@
             return carry
 
         lax.fori_loop(0, 2, heads, 0)
-        for slot, d, half, device in ((0, far, 0, z_up), (1, far, 1, z_down), (2, up, 1, z_up), (3, down, 0, z_down)):
+
+        def send_partial(slot, d, half, device):
             stage[b, slot] = project(d, half).astype(jnp.bfloat16)
             z_copy(b, slot, device).start()
+
+        send_partial(0, far, 0, z_up)
+        send_partial(1, far, 1, z_down)
+        pl.when(b > 0)(lambda: pass_on(b - 1))
+        send_partial(2, up, 1, z_up)
+        send_partial(3, down, 0, z_down)
+        hold[0] = project(up, 0)
+        hold[1] = project(down, 1)
         for half in range(2):
             own[pl.ds(pl.multiple_of(b * BS, BS), BS), half * HALF : (half + 1) * HALF] = project(z, half)
-        for slot, arrived, d, half, device in ((4, 0, up, 0, z_up), (5, 1, down, 1, z_down)):
-            part = project(d, half)
-            z_wait(b, arrived)
-            stage[b, slot] = (part + zrecv[b, arrived].astype(jnp.float32)).astype(jnp.bfloat16)
-            z_copy(b, slot, device).start()
         return carry
 
-    events = [
-        blocks.along_a, lambda: blocks.along_b(0), blocks.far_a,
-        lambda: blocks.along_b(-1), lambda: blocks.along_b(1), lambda: blocks.along_b(2),
-    ]
+    def forward(i):
+        for r in range(2):
+            pass_copy(r, i).wait_recv()
+            hand_on(r, i).start()
 
     def image_step(i, carry):
-        for k, event in enumerate(events):
-            pl.when(i == k)(event)
+        for k, n in enumerate((0, 2, 1, 3)):
+            pl.when(i == 2 * k)(lambda n=n: forward(n))
         image_part(i // 2, lax.rem(i, 2))
         return carry
 
     lax.fori_loop(0, 2 * BLOCKS, image_step, 0)
-    for da in A_STEPS:
-        blocks.far_b(da)
+    arrivals = [(r, k, i) for r in range(2) for k in range(4) for i in range(4) if (r, k) != (0, 0)]
+    for r, k, i in arrivals:
+        wait_for(got.at[origin(r, k, i)], got_recv.at[r, k, i])
     locals_[3].wait()
-    blocks.finish()
     lax.fori_loop(0, BLOCKS, one_block, 0)
+    pass_on(BLOCKS - 1)
 
     def last(b, carry):
         rows = pl.ds(pl.multiple_of(b * BS, BS), BS)
@@ -300,12 +411,20 @@
             total = own[rows, cols] + zrecv[b, one].astype(jnp.float32) + zrecv[b, two].astype(jnp.float32)
             out_ref[rows, cols] = total.astype(jnp.bfloat16)
         for slot in range(6):
-            pltpu.make_async_copy(stage.at[b, slot], stage.at[b, slot], z_send.at[b, slot]).wait()
+            wait_for(stage.at[b, slot], z_send.at[b, slot])
         return carry
 
     lax.fori_loop(0, BLOCKS, last, 0)
     images.drain()
-    blocks.drain()
+    for k, r in table_slots:
+        wait_for(table.at[0, 0], table_send.at[k, r])
+    for copy in row_copies:
+        copy.wait_send()
+    for r in range(2):
+        for i in range(4):
+            pass_copy(r, i).wait_send()
+    for r, k, i in arrivals:
+        wait_for(got.at[0], got_send.at[r, k, i])
 
 
 def body(queries, keys_values, image_kv, image_of, ancestors, counts, out_weight):
@@ -320,21 +439,36 @@
         in_specs=[smem] * 3 + [hbm] * 4,
         out_specs=pl.BlockSpec(memory_space=pltpu.VMEM),
         scratch_shapes=[
-            pltpu.VMEM((SEQ * BLOCKS, BS, KVW), bf16),
             pltpu.VMEM((SEQ * 2, BS, KVW), bf16),
             pltpu.VMEM(out_weight.shape, bf16),
             pltpu.VMEM(queries.shape, bf16),
             pltpu.VMEM((BLOCKS * UNITS, HEAD_DIM, ROWS), f32),
             pltpu.VMEM((BLOCKS * UNITS, 8, ROWS), f32),
             pltpu.VMEM((BS, HEADS * HEAD_DIM), bf16),
+            pltpu.VMEM((2, BS, HALF), f32),
             pltpu.VMEM((BLOCKS * BS, DSHARE), f32),
             pltpu.VMEM((BLOCKS, 6, BS, HALF), bf16),
             pltpu.VMEM((BLOCKS, 6, BS, HALF), bf16),
-            pltpu.SemaphoreType.DMA((4,)),
+            pltpu.VMEM((BLOCKS, BS, KVW), bf16),
+            pltpu.VMEM((BLOCKS, BS, KVW), bf16),
+            pltpu.VMEM((BLOCKS, BS, KVW), bf16),
+            pltpu.VMEM((BLOCKS, BS, KVW), bf16),
+            pltpu.VMEM((4, 2, 4, BS, KVW), bf16),
+            pltpu.VMEM((2, 4, BS, KVW), bf16),
+            pltpu.VMEM((SEQ, BS, KVW), bf16),
+            pltpu.VMEM((SIDE, 2, 8, 128), jnp.int32),
+            pltpu.SMEM((SIDE, 2, 8, 128), jnp.int32),
+            pltpu.SemaphoreType.DMA((5,)),
             pltpu.SemaphoreType.DMA((36,)),
             pltpu.SemaphoreType.DMA((36,)),
-            pltpu.SemaphoreType.DMA((36,)),
-            pltpu.SemaphoreType.DMA((36,)),
+            pltpu.SemaphoreType.DMA((6,)),
+            pltpu.SemaphoreType.DMA((6,)),
+            pltpu.SemaphoreType.DMA((2, 4)),
+            pltpu.SemaphoreType.DMA((2, 4)),
+            pltpu.SemaphoreType.DMA((2, 4, 4)),
+            pltpu.SemaphoreType.DMA((2, 4, 4)),
+            pltpu.SemaphoreType.DMA((SIDE, 2)),
+            pltpu.SemaphoreType.DMA((SIDE, 2)),
             pltpu.SemaphoreType.DMA((BLOCKS, 6)),
             pltpu.SemaphoreType.DMA((BLOCKS, 6)),
         ],

time: 139 us -> 118 us (0.85)
  Pallas kernels: 132 us -> 111 us
    pallas_call x1, Pallas kernels: 132 us -> 111 us  [body(): pl.pallas_call(kernel, out_shape=jax.ShapeDtypeStruct((BLOCKS * BS, DSHAR...]
where the time goes in v3:
time: 118 us; the launch traced here: 117 us
  Pallas kernels  111 us (94%)
  local copies, waits for them, and re-layouts  6.26 us (5%)
    pallas_call x1, Pallas kernels, body(): pl.pallas_call(kernel, out_shape=jax.ShapeDtypeStruct((BLOCKS * BS, DSHAR...  111 us

profile of v3, /device:TPU:0, one launch (start us, length us, event | category | flops | bytes accessed | tf_op | source)
XLA Modules:
  0.0 117.5 jit_solution(4731468437333114556)
XLA Ops:
  0.0 1.8 %reshape.7.im_in = bf16[2,128,512]{2,1,0:T(8,128)(2,1)} reshape(bf16[256,2,256]{2,1,0:T(2,128)(2,1)} %param.9) | data formatting | bytes 524288 | tf_op jit(solution)/shard_map/reshape | solution.py:432
  1.8 2.2 %reshape.6.kv_in = bf16[4,128,512]{2,1,0:T(8,128)(2,1)} reshape(bf16[512,2,256]{2,1,0:T(2,128)(2,1)} %param.8) | data formatting | bytes 1048576 | tf_op jit(solution)/shard_map/reshape | solution.py:431
  4.0 111.2 %tree_attention.1 = bf16[512,1024]{1,0:T(8,128)(2,1)} custom-call(s32[4]{0:T(128)} %image_of.1, s32[4,8]{1,0:T(4,128)} %ancestors.1, s32[4]{0:T(128)} %counts.1, bf16[512,2048]{1,0:T(8,128)(2,1)} %q_in.1, bf16[4,128,512]{2,1,0:T(8,128)(2,1)} %reshape.6.kv_in, bf16[2,128,512]{2,1,0:T(8,128)(2,1)} %reshape.7.im_in, bf16[2048,4096]{1,0:T(8,128)(2,1)} %w_in.1), custom_call_target="tpu_custom_call" | custom-call | tf_op jit(solution)/shard_map/tree_attention/pallas_call | solution.py:436
  115.2 2.3 %copy.9 = bf16[512,1024]{1,0:T(8,128)(2,1)} copy(bf16[512,1024]{1,0:T(8,128)(2,1)} %tree_attention.1) | data formatting | bytes 2097152

commit v4 on v3

--- a/solution.py
+++ b/solution.py
@@ -30,9 +30,9 @@
 
 def kernel(
     image_of, ancestors, counts, q_in, kv_in, im_in, w_in, out_ref,
-    im, w, q, acc, stat, att, hold, own, stage, zrecv,
+    kv_raw, im_raw, result, im, w, q, acc, stat, att, hold, own, stage, zrecv,
     row_own, row_prev, row_next, row_far, picked, passing, got, table, needs,
-    local_sem, im_send, im_recv, row_send, row_recv, pass_send, pass_recv, got_send, got_recv,
+    local_sem, out_sem, im_send, im_recv, row_send, row_recv, pass_send, pass_recv, got_send, got_recv,
     table_send, table_recv, z_send, z_recv,
 ):
     me = lax.axis_index("seq")
@@ -58,8 +58,8 @@
         near += [(chip(da, db, 0), z), (chip(da, db, 1), z)]
 
     locals_ = [
-        pltpu.make_async_copy(kv_in, row_own, local_sem.at[0]),
-        pltpu.make_async_copy(im_in, im.at[pl.ds(me * 2, 2)], local_sem.at[1]),
+        pltpu.make_async_copy(kv_in, kv_raw, local_sem.at[0]),
+        pltpu.make_async_copy(im_in, im_raw, local_sem.at[1]),
         pltpu.make_async_copy(q_in, q, local_sem.at[2]),
         pltpu.make_async_copy(w_in, w, local_sem.at[3]),
     ]
@@ -77,6 +77,20 @@
             block = jnp.full((8, 128), ancestors[b, a], jnp.int32)
             listed = jnp.maximum(listed, jnp.where((block >> 2) == lane, block & 3, 0))
     table[0, 0] = listed
+
+    to_row = lax.broadcasted_iota(jnp.int32, (2 * BS, 2 * BS), 0)
+    from_row = lax.broadcasted_iota(jnp.int32, (2 * BS, 2 * BS), 1)
+    wanted = jnp.where(to_row < BS, 2 * to_row, 2 * to_row - (2 * BS - 1))
+    parting = jnp.where(from_row == wanted, 1.0, 0.0).astype(jnp.bfloat16)
+    for raw, buf, first, count, copy in (
+        (im_raw, im, me * 2, 2, locals_[1]), (kv_raw, row_own, 0, BLOCKS, locals_[0]),
+    ):
+        copy.wait()
+        for n in range(count):
+            turns = raw[n * BS : (n + 1) * BS].reshape(2 * BS, KVW // 2)
+            parted = jnp.dot(parting, turns, preferred_element_type=jnp.float32).astype(jnp.bfloat16)
+            buf[first + n, :, : KVW // 2] = parted[:BS]
+            buf[first + n, :, KVW // 2 :] = parted[BS:]
 
     pl.semaphore_wait(barrier, len(near))
 
@@ -184,13 +198,13 @@
                 ref = self.buf.at[pl.ds(0, part)]
                 pltpu.make_async_copy(ref, ref, self.send.at[index]).wait()
 
-    images = Gather(im, im_in, 2, im_send, im_recv)
+    images = Gather(im, im.at[pl.ds(me * 2, 2)], 2, im_send, im_recv)
     low, high = pl.ds(0, 2), pl.ds(2, 2)
     row_copies = [
-        copy_to(kv_in.at[low], row_prev.at[low], row_send.at[0], row_recv.at[0], a_up),
-        copy_to(kv_in.at[high], row_next.at[high], row_send.at[1], row_recv.at[1], a_down),
-        copy_to(kv_in.at[high], row_prev.at[high], row_send.at[2], row_recv.at[2], a_up),
-        copy_to(kv_in.at[low], row_next.at[low], row_send.at[3], row_recv.at[3], a_down),
+        copy_to(row_own.at[low], row_prev.at[low], row_send.at[0], row_recv.at[0], a_up),
+        copy_to(row_own.at[high], row_next.at[high], row_send.at[1], row_recv.at[1], a_down),
+        copy_to(row_own.at[high], row_prev.at[high], row_send.at[2], row_recv.at[2], a_up),
+        copy_to(row_own.at[low], row_next.at[low], row_send.at[3], row_recv.at[3], a_down),
         copy_to(row_prev.at[low], row_far.at[low], row_send.at[4], row_recv.at[4], a_up),
         copy_to(row_next.at[high], row_far.at[high], row_send.at[5], row_recv.at[5], a_down),
     ]
@@ -237,7 +251,8 @@
         got[source] = row[needs[0, 0, 0, source]]
 
     images.begin()
-    row_begin()
+    row_copies[0].start()
+    row_copies[1].start()
     images.along_a()
     for k, r in table_slots:
         wait_for(table.at[k, r], table_recv.at[k, r])
@@ -245,23 +260,16 @@
     to_scalars.start()
     images.along_b(0)
     images.far_a()
+    row_copies[2].start()
+    row_copies[3].start()
     to_scalars.wait()
-    locals_[0].wait()
-    pick(0, row_own)
-    row_pass()
     for da in A_STEPS[1:]:
         images.along_b(da)
-    row_copies[2].wait_recv()
-    pick(1, row_prev)
-    row_copies[3].wait_recv()
-    pick(2, row_next)
+    pick(0, row_own)
     for da in A_STEPS:
         images.far_b(da)
-    row_copies[4].wait_recv()
-    row_copies[5].wait_recv()
-    pick(3, row_far)
-    for copy in locals_[1:3]:
-        copy.wait()
+    row_pass()
+    locals_[2].wait()
     images.finish()
 
     nt = (((1,), (1,)), ((), ()))
@@ -389,8 +397,21 @@
             hand_on(r, i).start()
 
     def image_step(i, carry):
-        for k, n in enumerate((0, 2, 1, 3)):
-            pl.when(i == 2 * k)(lambda n=n: forward(n))
+        def mid_pick():
+            row_copies[2].wait_recv()
+            pick(1, row_prev)
+            row_copies[3].wait_recv()
+            pick(2, row_next)
+
+        def last_pick():
+            row_copies[4].wait_recv()
+            row_copies[5].wait_recv()
+            pick(3, row_far)
+
+        pl.when(i == 0)(mid_pick)
+        pl.when(i == 1)(last_pick)
+        for step, n in ((2, 0), (2, 1), (3, 2), (4, 3)):
+            pl.when(i == step)(lambda n=n: forward(n))
         image_part(i // 2, lax.rem(i, 2))
         return carry
 
@@ -402,6 +423,10 @@
     lax.fori_loop(0, BLOCKS, one_block, 0)
     pass_on(BLOCKS - 1)
 
+    def out_copy(b):
+        rows = pl.ds(pl.multiple_of(b * BS, BS), BS)
+        return pltpu.make_async_copy(result.at[rows], out_ref.at[rows], out_sem.at[b])
+
     def last(b, carry):
         rows = pl.ds(pl.multiple_of(b * BS, BS), BS)
         for slot in (2, 3, 4, 5):
@@ -409,13 +434,16 @@
         for half, (one, two) in enumerate(((3, 4), (2, 5))):
             cols = slice(half * HALF, (half + 1) * HALF)
             total = own[rows, cols] + zrecv[b, one].astype(jnp.float32) + zrecv[b, two].astype(jnp.float32)
-            out_ref[rows, cols] = total.astype(jnp.bfloat16)
+            result[rows, cols] = total.astype(jnp.bfloat16)
+        out_copy(b).start()
         for slot in range(6):
             wait_for(stage.at[b, slot], z_send.at[b, slot])
         return carry
 
     lax.fori_loop(0, BLOCKS, last, 0)
     images.drain()
+    for b in range(BLOCKS):
+        out_copy(b).wait()
     for k, r in table_slots:
         wait_for(table.at[0, 0], table_send.at[k, r])
     for copy in row_copies:
@@ -428,8 +456,6 @@
 
 
 def body(queries, keys_values, image_kv, image_of, ancestors, counts, out_weight):
-    kv = keys_values.reshape(BLOCKS, BS, KVW)
-    im = image_kv.reshape(2, BS, KVW)
     smem = pl.BlockSpec(memory_space=pltpu.SMEM)
     hbm = pl.BlockSpec(memory_space=pl.ANY)
     bf16, f32 = jnp.bfloat16, jnp.float32
@@ -437,8 +463,11 @@
         kernel,
         out_shape=jax.ShapeDtypeStruct((BLOCKS * BS, DSHARE), bf16),
         in_specs=[smem] * 3 + [hbm] * 4,
-        out_specs=pl.BlockSpec(memory_space=pltpu.VMEM),
+        out_specs=hbm,
         scratch_shapes=[
+            pltpu.VMEM(keys_values.shape, bf16),
+            pltpu.VMEM(image_kv.shape, bf16),
+            pltpu.VMEM((BLOCKS * BS, DSHARE), bf16),
             pltpu.VMEM((SEQ * 2, BS, KVW), bf16),
             pltpu.VMEM(out_weight.shape, bf16),
             pltpu.VMEM(queries.shape, bf16),
@@ -459,6 +488,7 @@
             pltpu.VMEM((SIDE, 2, 8, 128), jnp.int32),
             pltpu.SMEM((SIDE, 2, 8, 128), jnp.int32),
             pltpu.SemaphoreType.DMA((5,)),
+            pltpu.SemaphoreType.DMA((BLOCKS,)),
             pltpu.SemaphoreType.DMA((36,)),
             pltpu.SemaphoreType.DMA((36,)),
             pltpu.SemaphoreType.DMA((6,)),
@@ -476,7 +506,7 @@
             collective_id=0, has_side_effects=True, vmem_limit_bytes=62 * 1024 * 1024
         ),
         name="tree_attention",
-    )(image_of, ancestors, counts, queries, kv, im, out_weight)
+    )(image_of, ancestors, counts, queries, keys_values, image_kv, out_weight)
 
 
 def solution(mesh):

time: 118 us -> 111 us (0.941)
  local copies, waits for them, and re-layouts: 6.26 us -> 2.26 us
  Pallas kernels: 111 us -> 108 us
    reshape x2 -> x0, local copies, waits for them, and re-layouts: 4 us -> none  [the longest x1 2.17 us: body(): kv = keys_values.reshape(BLOCKS, BS, KVW)]
    pallas_call x1, Pallas kernels: 111 us -> 108 us  [body(): pl.pallas_call(kernel, out_shape=jax.ShapeDtypeStruct((BLOCKS * BS, DSHAR...]
where the time goes in v4:
time: 111 us; the launch traced here: 110 us
  Pallas kernels  108 us (97%)
  local copies, waits for them, and re-layouts  2.26 us (2%)
    pallas_call x1, Pallas kernels, body(): pl.pallas_call(kernel, out_shape=jax.ShapeDtypeStruct((BLOCKS * BS, DSHAR...  108 us
    unnamed x1, local copies, waits for them, and re-layouts  2.26 us

profile of v4, /device:TPU:0, one launch (start us, length us, event | category | flops | bytes accessed | tf_op | source)
XLA Modules:
  0.0 110.1 jit_solution(15408159228581024586)
XLA Ops:
  0.0 107.8 %tree_attention.1 = bf16[512,1024]{1,0:T(8,128)(2,1)} custom-call(s32[4]{0:T(128)} %image_of.1, s32[4,8]{1,0:T(4,128)} %ancestors.1, s32[4]{0:T(128)} %counts.1, bf16[512,2048]{1,0:T(8,128)(2,1)} %q_in.1, bf16[512,2,256]{2,1,0:T(2,128)(2,1)} %kv_in.1, bf16[256,2,256]{2,1,0:T(2,128)(2,1)} %im_in.1, bf16[2048,4096]{1,0:T(8,128)(2,1)} %w_in.1), custom_call_target="tpu_custom_call" | custom-call | tf_op jit(solution)/shard_map/tree_attention/pallas_call | solution.py:462
  107.8 2.3 %copy.9 = bf16[512,1024]{1,0:T(8,128)(2,1)} copy(bf16[512,1024]{1,0:T(8,128)(2,1)} %tree_attention.1) | data formatting | bytes 2097152

commit v5 on v4

--- a/solution.py
+++ b/solution.py
@@ -16,8 +16,8 @@
 SEQ = 32
 KVW = 512
 HEADS = 16
-GROUP = 4
-UNITS = HEADS // GROUP
+GROUP = 8
+KV_HEADS = HEADS // GROUP
 ROWS = GROUP * BS
 DSHARE = 1024
 HALF = 512
@@ -285,67 +285,56 @@
         ]
         return jnp.concatenate([q[rows, cols] for cols in lanes], axis=0)
 
-    def lanes_of(j):
-        return (
-            pl.ds(pl.multiple_of(j * HEAD_DIM, HEAD_DIM), HEAD_DIM),
-            pl.ds(pl.multiple_of(256 + j * HEAD_DIM, HEAD_DIM), HEAD_DIM),
-        )
+    def heads_of(blocks, j):
+        k = jnp.concatenate([ref[i, :, j * HEAD_DIM : (j + 1) * HEAD_DIM] for ref, i in blocks], axis=0)
+        at = 256 + j * HEAD_DIM
+        v = jnp.concatenate([ref[i, :, at : at + HEAD_DIM] for ref, i in blocks], axis=0)
+        return k, jnp.concatenate([v.T, jnp.ones((16, v.shape[0]), jnp.bfloat16)], axis=0)
 
     key_at = lax.broadcasted_iota(jnp.int32, (BS, ROWS), 0)
     token_at = lax.broadcasted_iota(jnp.int32, (BS, ROWS), 1) & (BS - 1)
 
-    def image_part(b, j):
-        lanes = lanes_of(j)
+    def image_part(b):
         image = image_of[b]
-        k, v = (
-            jnp.concatenate(
-                [im[image * 8 + t, :, cols] for t in range(IMG_TOK // BS)] + [row_own[b, :, cols]], axis=0
-            )
-            for cols in lanes
-        )
-        v = v.T
-        for r in range(2):
-            u = 2 * j + r
-            slot = b * UNITS + u
-            s = dot(k, queries_of(b, u), nt)
-            s, s_own = s[:IMG_TOK], s[IMG_TOK:]
+        blocks = [(im, image * 8 + t) for t in range(IMG_TOK // BS)] + [(row_own, b)]
+        heads = [heads_of(blocks, j) for j in range(KV_HEADS)]
+        scores = [dot(heads[j][0], queries_of(b, j), nt) for j in range(KV_HEADS)]
+        for j in range(KV_HEADS):
+            slot = b * KV_HEADS + j
+            s, s_own = scores[j][:IMG_TOK], scores[j][IMG_TOK:]
             s_own = jnp.where(key_at <= token_at, s_own, -BIG)
             top = jnp.maximum(jnp.max(s, axis=0, keepdims=True), jnp.max(s_own, axis=0, keepdims=True))
-            e = jnp.exp2((s - top) * SCALE2)
-            e_own = jnp.exp2((s_own - top) * SCALE2)
+            e = jnp.exp2((s - top) * SCALE2).astype(jnp.bfloat16)
+            e_own = jnp.exp2((s_own - top) * SCALE2).astype(jnp.bfloat16)
+            o = dot(heads[j][1], jnp.concatenate([e, e_own], axis=0), nn)
             stat[slot, 0:1] = top
-            stat[slot, 1:2] = jnp.sum(e, axis=0, keepdims=True) + jnp.sum(e_own, axis=0, keepdims=True)
-            acc[slot] = dot(v, jnp.concatenate([e.astype(jnp.bfloat16), e_own.astype(jnp.bfloat16)], axis=0), nn)
-
-    def rest_part(b, j):
-        k_lanes, v_lanes = lanes_of(j)
+            stat[slot, 1:2] = o[HEAD_DIM : HEAD_DIM + 1]
+            acc[slot] = o[:HEAD_DIM]
+
+    def rest_part(b):
         live = jnp.full((1, ROWS), counts[b], jnp.int32)
-        at = [lax.shift_right_logical(ancestors[b, a], 2) for a in range(ANC)]
-        k = jnp.concatenate([got[i, :, k_lanes] for i in at], axis=0)
-        v = jnp.concatenate([got[i, :, v_lanes] for i in at], axis=0).T
-        for r in range(2):
-            u = 2 * j + r
-            slot = b * UNITS + u
-            s = dot(k, queries_of(b, u), nt)
-            parts = [s[a * BS : (a + 1) * BS] for a in range(ANC)]
+        blocks = [(got, lax.shift_right_logical(ancestors[b, a], 2)) for a in range(ANC)]
+        heads = [heads_of(blocks, j) for j in range(KV_HEADS)]
+        scores = [dot(heads[j][0], queries_of(b, j), nt) for j in range(KV_HEADS)]
+        for j in range(KV_HEADS):
+            slot = b * KV_HEADS + j
+            parts = [scores[j][a * BS : (a + 1) * BS] for a in range(ANC)]
             before = stat[slot, 0:1]
             top = before
             for a in range(ANC):
                 best = jnp.max(parts[a], axis=0, keepdims=True)
                 top = jnp.maximum(top, jnp.where(live > a, best, -BIG))
             keep = jnp.exp2((before - top) * SCALE2)
-            total = stat[slot, 1:2] * keep
             weights = []
             for a in range(ANC):
                 under = jnp.where(live > a, top, BIG)
-                e = jnp.exp2((parts[a] - under) * SCALE2)
-                total = total + jnp.sum(e, axis=0, keepdims=True)
-                weights.append(e.astype(jnp.bfloat16))
-            o = acc[slot] * keep + dot(v, jnp.concatenate(weights, axis=0), nn)
-            o = o / total
+                weights.append(jnp.exp2((parts[a] - under) * SCALE2).astype(jnp.bfloat16))
+            o = dot(heads[j][1], jnp.concatenate(weights, axis=0), nn)
+            total = stat[slot, 1:2] * keep + o[HEAD_DIM : HEAD_DIM + 1]
+            o = (acc[slot] * keep + o[:HEAD_DIM]) / total
             for h in range(GROUP):
-                cols = pl.ds(pl.multiple_of((u * GROUP + h) * HEAD_DIM, HEAD_DIM), HEAD_DIM)
-                att[:, cols] = o[:, h * BS : (h + 1) * BS].T.astype(jnp.bfloat16)
+                at = (j * GROUP + h) * HEAD_DIM
+                att[:, at : at + HEAD_DIM] = o[:, h * BS : (h + 1) * BS].T.astype(jnp.bfloat16)
 
     def project(d, half):
         cols = pl.ds(pl.multiple_of(d * DSHARE + half * HALF, HALF), HALF)
@@ -370,11 +359,7 @@
             z_copy(b, slot, device).start()
 
     def one_block(b, carry):
-        def heads(j, carry):
-            rest_part(b, j)
-            return carry
-
-        lax.fori_loop(0, 2, heads, 0)
+        rest_part(b)
 
         def send_partial(slot, d, half, device):
             stage[b, slot] = project(d, half).astype(jnp.bfloat16)
@@ -410,12 +395,12 @@
 
         pl.when(i == 0)(mid_pick)
         pl.when(i == 1)(last_pick)
-        for step, n in ((2, 0), (2, 1), (3, 2), (4, 3)):
+        for step, n in ((1, 0), (1, 1), (2, 2), (3, 3)):
             pl.when(i == step)(lambda n=n: forward(n))
-        image_part(i // 2, lax.rem(i, 2))
+        image_part(i)
         return carry
 
-    lax.fori_loop(0, 2 * BLOCKS, image_step, 0)
+    lax.fori_loop(0, BLOCKS, image_step, 0)
     arrivals = [(r, k, i) for r in range(2) for k in range(4) for i in range(4) if (r, k) != (0, 0)]
     for r, k, i in arrivals:
         wait_for(got.at[origin(r, k, i)], got_recv.at[r, k, i])
@@ -471,8 +456,8 @@
             pltpu.VMEM((SEQ * 2, BS, KVW), bf16),
             pltpu.VMEM(out_weight.shape, bf16),
             pltpu.VMEM(queries.shape, bf16),
-            pltpu.VMEM((BLOCKS * UNITS, HEAD_DIM, ROWS), f32),
-            pltpu.VMEM((BLOCKS * UNITS, 8, ROWS), f32),
+            pltpu.VMEM((BLOCKS * KV_HEADS, HEAD_DIM, ROWS), f32),
+            pltpu.VMEM((BLOCKS * KV_HEADS, 8, ROWS), f32),
             pltpu.VMEM((BS, HEADS * HEAD_DIM), bf16),
             pltpu.VMEM((2, BS, HALF), f32),
             pltpu.VMEM((BLOCKS * BS, DSHARE), f32),

time: 111 us -> 108 us (0.973)
  Pallas kernels: 108 us -> 105 us
    pallas_call x1, Pallas kernels: 108 us -> 105 us  [body(): pl.pallas_call(kernel, out_shape=jax.ShapeDtypeStruct((BLOCKS * BS, DSHAR...]
where the time goes in v5:
time: 108 us; the launch traced here: 107 us
  Pallas kernels  105 us (97%)
  local copies, waits for them, and re-layouts  2.26 us (2%)
    pallas_call x1, Pallas kernels, body(): pl.pallas_call(kernel, out_shape=jax.ShapeDtypeStruct((BLOCKS * BS, DSHAR...  105 us
    unnamed x1, local copies, waits for them, and re-layouts  2.26 us

profile of v5, /device:TPU:0, one launch (start us, length us, event | category | flops | bytes accessed | tf_op | source)
XLA Modules:
  0.0 106.9 jit_solution(10505293529979265673)
XLA Ops:
  0.0 104.6 %tree_attention.1 = bf16[512,1024]{1,0:T(8,128)(2,1)} custom-call(s32[4]{0:T(128)} %image_of.1, s32[4,8]{1,0:T(4,128)} %ancestors.1, s32[4]{0:T(128)} %counts.1, bf16[512,2048]{1,0:T(8,128)(2,1)} %q_in.1, bf16[512,2,256]{2,1,0:T(2,128)(2,1)} %kv_in.1, bf16[256,2,256]{2,1,0:T(2,128)(2,1)} %im_in.1, bf16[2048,4096]{1,0:T(8,128)(2,1)} %w_in.1), custom_call_target="tpu_custom_call" | custom-call | tf_op jit(solution)/shard_map/tree_attention/pallas_call | solution.py:447
  104.6 2.3 %copy.9 = bf16[512,1024]{1,0:T(8,128)(2,1)} copy(bf16[512,1024]{1,0:T(8,128)(2,1)} %tree_attention.1) | data formatting | bytes 2097152

commit v6 on v5

--- a/solution.py
+++ b/solution.py
@@ -406,6 +406,16 @@
         wait_for(got.at[origin(r, k, i)], got_recv.at[r, k, i])
     locals_[3].wait()
     lax.fori_loop(0, BLOCKS, one_block, 0)
+    images.drain()
+    for k, r in table_slots:
+        wait_for(table.at[0, 0], table_send.at[k, r])
+    for copy in row_copies:
+        copy.wait_send()
+    for r in range(2):
+        for i in range(4):
+            pass_copy(r, i).wait_send()
+    for r, k, i in arrivals:
+        wait_for(got.at[0], got_send.at[r, k, i])
     pass_on(BLOCKS - 1)
 
     def out_copy(b):
@@ -421,23 +431,14 @@
             total = own[rows, cols] + zrecv[b, one].astype(jnp.float32) + zrecv[b, two].astype(jnp.float32)
             result[rows, cols] = total.astype(jnp.bfloat16)
         out_copy(b).start()
+        return carry
+
+    lax.fori_loop(0, BLOCKS, last, 0)
+    for b in range(BLOCKS):
         for slot in range(6):
             wait_for(stage.at[b, slot], z_send.at[b, slot])
-        return carry
-
-    lax.fori_loop(0, BLOCKS, last, 0)
-    images.drain()
     for b in range(BLOCKS):
         out_copy(b).wait()
-    for k, r in table_slots:
-        wait_for(table.at[0, 0], table_send.at[k, r])
-    for copy in row_copies:
-        copy.wait_send()
-    for r in range(2):
-        for i in range(4):
-            pass_copy(r, i).wait_send()
-    for r, k, i in arrivals:
-        wait_for(got.at[0], got_send.at[r, k, i])
 
 
 def body(queries, keys_values, image_kv, image_of, ancestors, counts, out_weight):

time: 108 us -> 108 us (level)
  no operation moved by 1% of the time
where the time goes in v6:
time: 108 us; the launch traced here: 107 us
  Pallas kernels  105 us (97%)
  local copies, waits for them, and re-layouts  2.26 us (2%)
    pallas_call x1, Pallas kernels, body(): pl.pallas_call(kernel, out_shape=jax.ShapeDtypeStruct((BLOCKS * BS, DSHAR...  105 us
    unnamed x1, local copies, waits for them, and re-layouts  2.26 us

profile of v6, /device:TPU:0, one launch (start us, length us, event | category | flops | bytes accessed | tf_op | source)
XLA Modules:
  0.0 106.8 jit_solution(6718552571114755146)
XLA Ops:
  0.0 104.5 %tree_attention.1 = bf16[512,1024]{1,0:T(8,128)(2,1)} custom-call(s32[4]{0:T(128)} %image_of.1, s32[4,8]{1,0:T(4,128)} %ancestors.1, s32[4]{0:T(128)} %counts.1, bf16[512,2048]{1,0:T(8,128)(2,1)} %q_in.1, bf16[512,2,256]{2,1,0:T(2,128)(2,1)} %kv_in.1, bf16[256,2,256]{2,1,0:T(2,128)(2,1)} %im_in.1, bf16[2048,4096]{1,0:T(8,128)(2,1)} %w_in.1), custom_call_target="tpu_custom_call" | custom-call | tf_op jit(solution)/shard_map/tree_attention/pallas_call | solution.py:448
  104.5 2.3 %copy.9 = bf16[512,1024]{1,0:T(8,128)(2,1)} copy(bf16[512,1024]{1,0:T(8,128)(2,1)} %tree_attention.1) | data formatting | bytes 2097152
